TPU v7x, 512 devices: a whole 4x4x16 slice. The times are simulated.
512 devices in a mesh: sector: 32 (over z, core), chan: 16 (over x, y).
Axes of the slice: x: 4, y: 4, z: 16, core: 2. Of those that a mesh axis runs over, the one named last changes fastest.
Arguments:
- wavefunc: float32 [128, 256, 256], P('sector', 'chan'), may hold values from -6 to 6
- left_env: float32 [32, 128, 256, 256], P('chan', 'sector'), may hold values from -0.375 to 0.375
- right_env: float32 [32, 128, 256, 256], P('chan', 'sector'), may hold values from -0.375 to 0.375
- source: int32 [5, 128], replicated, may hold values from 0 to 127, as said below
- shift_class: int32 [32], replicated, may hold values from 0 to 4
- channel_block_mask: int32 [32, 128], replicated, may hold values 0 or 1
- block_size: int32 [128], replicated, may hold values from 128 to 256
Outputs:
- sigma: float32 [128, 256, 256], P('sector', 'chan')
Inputs may be any that keep to these rules, and one draw needn't show every extreme that they name: source[q, t] differs from t by at most 4.
All inputs are finite; a program needn't handle non-finite values.
Results may differ from a plain program's by a relative error of at most 0.0001.
Values sent between devices are 32-bit elements; how exact they have to be, the bound alone decides.
A program may use at most 64 MiB of HBM per device.

v0:
```python
import jax
import jax.numpy as jnp
from jax import lax
from jax.sharding import PartitionSpec as P


def padded(block, sides, width):
    for axis, dim in sides:
        count = lax.axis_size(axis)
        forward = [(i, i + 1) for i in range(count - 1)]
        backward = [(target, source) for source, target in forward]
        low = lax.ppermute(
            lax.slice_in_dim(block, block.shape[dim] - width, None, axis=dim), axis, forward
        )
        high = lax.ppermute(lax.slice_in_dim(block, 0, width, axis=dim), axis, backward)
        block = jnp.concatenate([low, block, high], axis=dim)
    return block


def body(wavefunc, left_env, right_env, source, shift_class, channel_block_mask, block_size):
    sec_local = wavefunc.shape[0]
    block = wavefunc.shape[2]
    chan_local = left_env.shape[0]
    chan_count = lax.axis_size("chan")
    sector_index = lax.axis_index("sector")
    chan_index = lax.axis_index("chan")
    whole = lax.all_gather(wavefunc, "chan", axis=1, tiled=True)
    extended = padded(whole, (("sector", 0),), sec_local)
    targets = sector_index * sec_local + jnp.arange(sec_local, dtype=jnp.int32)
    channels = chan_index * chan_local + jnp.arange(chan_local, dtype=jnp.int32)
    kinds = jnp.take(shift_class, channels)
    sources = source[kinds[:, None], targets[None, :]]
    local_position = sources - (sector_index * sec_local - sec_local)
    positions = jnp.arange(block, dtype=jnp.int32)
    source_size = jnp.take(block_size, sources)
    source_live = jnp.logical_and(
        positions[None, None, :, None] < source_size[:, :, None, None],
        positions[None, None, None, :] < source_size[:, :, None, None],
    ).astype(jnp.float32)
    chosen = jnp.take(extended, local_position, axis=0) * source_live
    inner_product = jnp.einsum("wtab,wtbc->wtac", left_env, chosen, precision=lax.Precision.HIGHEST)
    outer_product = jnp.einsum(
        "wtac,wtcd->wtad", inner_product, right_env, precision=lax.Precision.HIGHEST
    )
    weights = channel_block_mask[channels[:, None], targets[None, :]].astype(jnp.float32)
    partial_sum = jnp.sum(outer_product * weights[:, :, None, None], axis=0)
    target_size = jnp.take(block_size, targets)
    target_live = jnp.logical_and(
        positions[None, :, None] < target_size[:, None, None],
        positions[None, None, :] < target_size[:, None, None],
    ).astype(jnp.float32)
    partial_sum = partial_sum * target_live / jnp.sqrt(jnp.float32(chan_local * chan_count))
    return lax.psum_scatter(partial_sum, "chan", scatter_dimension=1, tiled=True)


def solution(mesh):
    return jax.shard_map(
        body,
        mesh=mesh,
        in_specs=(
            P("sector", "chan", None),
            P("chan", "sector", None, None),
            P("chan", "sector", None, None),
            P(),
            P(),
            P(),
            P(),
        ),
        out_specs=P("sector", "chan", None),
        check_vma=False,
    )
```

profile of v0, /device:TPU:1, one launch (start us, length us, event | category | flops | bytes accessed | tf_op | source)
XLA Modules:
  0.0 201.4 jit_solution(16670600088292109853)
XLA Ops:
  6.5 0.7 all-gather.2.cloned.1.call-update
  7.3 1.3 gather_fusion.1
  8.7 0.1 reshape.217
  8.8 1.3 gather_fusion.2
  10.2 0.1 gather.27
  10.2 0.1 reshape.225
  10.4 1.3 gather_fusion
  11.7 60.6 %all-gather.2.cloned.1.call-done = f32[4,256,256]{2,1,0:T(8,128)} async-done(((f32[4,16,256]{2,1,0:T(8,128)}), f32[4,256,256]{2,1,0:T(8,128)}) %all-gather.2.cloned.1.call-update) | async-done | bytes 1048592 | tf_op jit(solution)/shard_map/all_gather | solution.py:27
  72.4 4.1 %collective-permute-start.1 = (f32[4,256,256]{2,1,0:T(8,128)}, f32[4,256,256]{2,1,0:T(8,128)}, u32[]{:S(2)}, u32[]{:S(2)}) collective-permute-start(f32[4,256,256]{2,1,0:T(8,128)} %all-gather.2.cloned.1.call-done), channel_id=1, source_target_pairs={{16,0},{32,16},{48,32},{64,48},{80,64},{96,80},{112,96},{128,112},... | collective-permute-start | bytes 3145736 | tf_op jit(solution)/shard_map/ppermute | solution.py:15
  76.5 3.1 %collective-permute-start = (f32[4,256,256]{2,1,0:T(8,128)}, f32[4,256,256]{2,1,0:T(8,128)}, u32[]{:S(2)}, u32[]{:S(2)}) collective-permute-start(f32[4,256,256]{2,1,0:T(8,128)} %all-gather.2.cloned.1.call-done), channel_id=1, source_target_pairs={{0,16},{16,32},{32,48},{48,64},{64,80},{80,96},{96,112},{112,128},... | collective-permute-start | bytes 3145736 | tf_op jit(solution)/shard_map/ppermute | solution.py:12
  79.6 0.1 reshape.220
  79.7 0.1 reshape.233
  79.8 0.6 gather_fusion.3
  80.4 0.1 reshape.224
  80.6 0.6 gather_fusion.5
  81.2 0.1 reshape.248
  81.5 8.9 %collective-permute-done.1 = f32[4,256,256]{2,1,0:T(8,128)} collective-permute-done((f32[4,256,256]{2,1,0:T(8,128)}, f32[4,256,256]{2,1,0:T(8,128)}, u32[]{:S(2)}, u32[]{:S(2)}) %collective-permute-start.1) | collective-permute-done | bytes 1048608 | tf_op jit(solution)/shard_map/ppermute | solution.py:15
  90.4 1.2 collective-permute-done
  91.6 3.5 %pad_maximum_fusion = f32[12,256,256]{2,1,0:T(8,128)} fusion(f32[4,256,256]{2,1,0:T(8,128)} %collective-permute-done.1, f32[4,256,256]{2,1,0:T(8,128)S(1)} %copy-done.4, f32[4,256,256]{2,1,0:T(8,128)} %collective-permute-done), kind=kLoop, calls=%fused_computation.6 | loop fusion | flops 1572864 | bytes 6291456 | tf_op jit(solution)/shard_map/concatenate | solution.py:16
  95.2 3.9 %gather_fusion.4 = f32[8,256,256]{2,1,0:T(8,128)} fusion(f32[12,256,256]{2,1,0:T(8,128)} %pad_maximum_fusion, s32[1024]{0:T(1024)S(1)} %pad_clamp_fusion), kind=kCustom, calls=%fused_computation.4 | custom fusion | bytes 4194336 | tf_op jit(solution)/shard_map/jit(_take)/gather | solution.py:40
  99.1 4.1 %fusion = f32[2,4,256,256]{2,3,1,0:T(8,128)S(1)} fusion(f32[2,4,256,256]{3,2,1,0:T(8,128)S(1)} %copy-done, f32[2,4,256,256]{3,2,1,0:T(8,128)} %bitcast.16, pred[2,4]{1,0:T(4,128)(4,1)S(1)} %compare_and_fusion, pred[2,4,256]{2,1,0:T(4,128)(4,1)S(1)} %iota_compare_fusion), kind=kOutput, calls=%fused_computation.8 | convolution fusion | flops 1612185600 | bytes 6293512 | tf_op jit(solution)/shard_map/wtab,wtbc->wtac/dot_general | solution.py:41
  103.2 2.2 %multiply_reduce_fusion = f32[4,256,256]{2,1,0:T(8,128)S(1)} fusion(f32[2,4,256,256]{2,3,1,0:T(8,128)S(1)} %fusion, f32[2,4,256,256]{3,2,1,0:T(8,128)S(1)} %copy-done.3, f32[2,4]{1,0:T(2,128)S(1)} %reshape.248), kind=kOutput, calls=%fused_computation.7 | convolution fusion | flops 1611399168 | bytes 5242912 | tf_op jit(solution)/shard_map/wtac,wtcd->wtad/dot_general | solution.py:42
  105.4 1.2 select_multiply_fusion
  106.6 87.9 %reduce-scatter.2.cloned.1.call-done = f32[4,16,256]{2,1,0:T(8,128)} async-done(((f32[4,256,256]{2,1,0:T(8,128)}), f32[4,16,256]{2,1,0:T(8,128)}) %reduce-scatter.2.cloned.1.call-update) | async-done | bytes 65552 | tf_op jit(solution)/shard_map/reduce_scatter | solution.py:53
  (31 shorter events, 0.5 us)
Async XLA Ops:
  6.5 92.5 %copy-start = (f32[2,4,256,256]{3,2,1,0:T(8,128)S(1)}, f32[2,4,256,256]{3,2,1,0:T(8,128)}, u32[]{:S(2)}) copy-start(f32[2,4,256,256]{3,2,1,0:T(8,128)} %param.8) | copy-start | bytes 6291460
  6.5 73.2 %copy-start.1 = (s32[128]{0:T(128)S(1)}, s32[128]{0:T(128)}, u32[]{:S(2)}) copy-start(s32[128]{0:T(128)} %param.13) | copy-start | bytes 1540
  6.5 74.0 %copy-start.2 = (s32[32,128]{1,0:T(8,128)S(1)}, s32[32,128]{1,0:T(8,128)}, u32[]{:S(2)}) copy-start(s32[32,128]{1,0:T(8,128)} %param.12) | copy-start | bytes 49156
  6.5 65.8 %all-gather.2.cloned.1.call-start = ((), (), s32[]{:S(2)}) async-start(), calls=%async_computation.1 | async-start | bytes 1114112 | tf_op jit(solution)/shard_map/all_gather | solution.py:27
  7.3 187.3 %reduce-scatter.2.cloned.1.call-start = ((), (), s32[]{:S(2)}) async-start(), calls=%async_computation.2 | async-start | bytes 1114112 | tf_op jit(solution)/shard_map/reduce_scatter | solution.py:53
  72.4 19.3 %copy-start.4 = (f32[4,256,256]{2,1,0:T(8,128)S(1)}, f32[4,256,256]{2,1,0:T(8,128)}, u32[]{:S(2)}) copy-start(f32[4,256,256]{2,1,0:T(8,128)} %all-gather.2.cloned.1.call-done) | copy-start | bytes 3145732
  72.4 18.1 %collective-permute-start.1 = (f32[4,256,256]{2,1,0:T(8,128)}, f32[4,256,256]{2,1,0:T(8,128)}, u32[]{:S(2)}, u32[]{:S(2)}) collective-permute-start(f32[4,256,256]{2,1,0:T(8,128)} %all-gather.2.cloned.1.call-done), channel_id=1, source_target_pairs={{16,0},{32,16},{48,32},{64,48},{80,64},{96,80},{112,96},{128,112},... | collective-permute-start | bytes 3145736 | tf_op jit(solution)/shard_map/ppermute | solution.py:15
  76.5 15.1 %collective-permute-start = (f32[4,256,256]{2,1,0:T(8,128)}, f32[4,256,256]{2,1,0:T(8,128)}, u32[]{:S(2)}, u32[]{:S(2)}) collective-permute-start(f32[4,256,256]{2,1,0:T(8,128)} %all-gather.2.cloned.1.call-done), channel_id=1, source_target_pairs={{0,16},{16,32},{32,48},{48,64},{64,80},{80,96},{96,112},{112,128},... | collective-permute-start | bytes 3145736 | tf_op jit(solution)/shard_map/ppermute | solution.py:12
  99.1 4.1 %copy-start.3 = (f32[2,4,256,256]{3,2,1,0:T(8,128)S(1)}, f32[2,4,256,256]{3,2,1,0:T(8,128)}, u32[]{:S(2)}) copy-start(f32[2,4,256,256]{3,2,1,0:T(8,128)} %param.9) | copy-start | bytes 6291460
Sparse Core Ops, SparseCore 0:
  10.4 61.8 all-gather.1
  106.7 87.7 reduce-scatter.1
where the time goes:
time: 202 us; the launch traced here: 201 us
  waiting for transfers between devices  159 us (79%)
  between operations  13.5 us (7%)
  local copies, waits for them, and re-layouts  9.79 us (5%)
  starting transfers between devices  7.26 us (4%)
  matrix products  6.32 us (3%)
  other arithmetic  5.11 us (3%)
    reduce_scatter x1, waiting for transfers between devices, body(): lax.psum_scatter(partial_sum, 'chan', scatter_dimension=1, tiled=True)  87.9 us
    all_gather x1, waiting for transfers between devices, body(): whole = lax.all_gather(wavefunc, 'chan', axis=1, tiled=True)  60.6 us
    ppermute x1, waiting for transfers between devices, padded(): lax.ppermute(lax.slice_in_dim(block, 0, width, axis=dim), axis, backward)  8.95 us
    ppermute x1, starting transfers between devices, padded(): lax.ppermute(lax.slice_in_dim(block, 0, width, axis=dim), axis, backward)  4.13 us
    dot_general x1, matrix products, body(): jnp.einsum('wtab,wtbc->wtac', left_env, chosen, precision=lax.Precision.H...  4.08 us
  transfers between devices with their start and end apart: 4, of which 4 were waited for; matrix products, arithmetic and copies ran while one was open for 3% of the time, Pallas kernels for 0%

commit v1 on v0

v1 whole, which is shorter than its diff:
```python
import functools

import jax
import jax.numpy as jnp
from jax import lax
from jax.experimental import pallas as pl
from jax.experimental.pallas import tpu as pltpu
from jax.sharding import PartitionSpec as P

MESH = pl.DeviceIdType.MESH
STEPS = (1, 3, 2)


def split(value):
    high = value.astype(jnp.bfloat16)
    low = (value - high.astype(jnp.float32)).astype(jnp.bfloat16)
    return high, low


def product(a_high, a_low, b_high, b_low):
    dot = functools.partial(jnp.dot, preferred_element_type=jnp.float32)
    return dot(a_high, b_high) + dot(a_high, b_low) + dot(a_low, b_high)


def kernel(
    wave, left, right, source, shift, mask, size, out,
    gathered, left_f, right_f, left_h, left_l, right_h, right_l,
    part, got, mid, got2, source_s, shift_s, mask_s, size_s,
    local_sem, x1s, x1r, y1s, y1r, x2s, x2r, y2s, y2r, zs, zr, cs, cr,
    rs1, rr1, rs2, rr2,
):
    sector = lax.axis_index("sector")
    chan = lax.axis_index("chan")
    z, core = sector // 2, lax.rem(sector, 2)
    x, y = chan // 4, lax.rem(chan, 4)

    x_at = [lax.rem(x + d, 4) for d in range(4)]
    y_at = [lax.rem(y + d, 4) for d in range(4)]
    x_peer = {d: (sector, x_at[d] * 4 + y) for d in STEPS}
    y_peer = {d: (sector, x * 4 + y_at[d]) for d in STEPS}
    twin = (z * 2 + 1 - core, chan)
    near = (lax.rem(sector + 2 * core - 1 + 32, 32), chan)
    own, next_base = 4, 8 * core
    twin_there, near_there = 8 * core, 8 - 8 * core

    loads = [
        pltpu.make_async_copy(source, source_s, local_sem.at[0]),
        pltpu.make_async_copy(shift, shift_s, local_sem.at[1]),
        pltpu.make_async_copy(mask, mask_s, local_sem.at[2]),
        pltpu.make_async_copy(size, size_s, local_sem.at[3]),
        pltpu.make_async_copy(left, left_f, local_sem.at[4]),
        pltpu.make_async_copy(right, right_f, local_sem.at[5]),
    ]
    keep = pltpu.make_async_copy(wave, gathered.at[pl.ds(own, 4), x, y], local_sem.at[6])
    keep.start()

    barrier = pltpu.get_barrier_semaphore()
    partners = [x_peer[d] for d in STEPS] + [y_peer[d] for d in STEPS] + [twin, near]
    for partner in partners:
        pl.semaphore_signal(barrier, inc=1, device_id=partner, device_id_type=MESH)
    for load in loads:
        load.start()
    keep.wait()
    pl.semaphore_wait(barrier, len(partners))

    waits = []

    def send(view, there, send_sem, recv_sem, device):
        copy = pltpu.make_async_remote_copy(
            src_ref=view, dst_ref=there, send_sem=send_sem, recv_sem=recv_sem,
            device_id=device, device_id_type=MESH,
        )
        copy.start()
        waits.append(copy)
        return copy

    def first(q, base):
        a, b = {}, {}
        for d in STEPS:
            ref = gathered.at[pl.ds(base, 2), x, y]
            a[d] = send(ref, ref, x1s.at[q, d - 1], x1r.at[q, d - 1], x_peer[d])
            ref = gathered.at[pl.ds(base + 2, 2), x, y]
            b[d] = send(ref, ref, y1s.at[q, d - 1], y1r.at[q, d - 1], y_peer[d])
        return a, b

    def second(q, base, e):
        found = []
        for d in STEPS:
            ref = gathered.at[pl.ds(base, 2), x_at[(4 - e) % 4], y]
            a = send(ref, ref, y2s.at[q, e, d - 1], y2r.at[q, e, d - 1], y_peer[d])
            ref = gathered.at[pl.ds(base + 2, 2), x, y_at[(4 - e) % 4]]
            b = send(ref, ref, x2s.at[q, e, d - 1], x2r.at[q, e, d - 1], x_peer[d])
            found.append((d, a, b))
        return found

    o1 = first(0, own)
    ref = gathered.at[pl.ds(own, 4), x, y]
    over = send(ref, gathered.at[pl.ds(near_there, 4), x, y], zs.at[0], zr.at[0], near)
    o2 = {0: second(0, own, 0)}
    for d in STEPS:
        o1[0][d].wait_recv()
        o1[1][d].wait_recv()
        o2[d] = second(0, own, d)
    over.wait_recv()
    n1 = first(1, next_base)
    n2 = {0: second(1, next_base, 0)}
    for d in STEPS:
        n1[0][d].wait_recv()
        n1[1][d].wait_recv()
        n2[d] = second(1, next_base, d)

    twins = []

    def to_twin(i, first_block, blocks, at_x, at_y):
        ref = gathered.at[pl.ds(own + first_block, blocks), at_x, at_y]
        there = gathered.at[pl.ds(twin_there + first_block, blocks), at_x, at_y]
        twins.append(send(ref, there, cs.at[i], cr.at[i], twin))

    every = pl.ds(0, 4)
    to_twin(0, 0, 2, every, y)
    to_twin(1, 2, 2, x, every)
    for i, d in enumerate(STEPS):
        for e in (0,) + STEPS:
            for step, a, b in o2[e]:
                if step == d:
                    a.wait_recv()
                    b.wait_recv()
        to_twin(2 + 2 * i, 0, 2, every, y_at[4 - d])
        to_twin(3 + 2 * i, 2, 2, x_at[4 - d], every)

    for load in loads:
        load.wait()
    for w in range(2):
        for t in range(4):
            left_h[w, t], left_l[w, t] = split(left_f[w, t])
            right_h[w, t], right_l[w, t] = split(right_f[w, t])

    for e in (0,) + STEPS:
        for step, a, b in n2[e]:
            a.wait_recv()
            b.wait_recv()
    for copy in twins:
        copy.wait_recv()

    rows = lax.broadcasted_iota(jnp.int32, (256, 256), 0)
    cols = lax.broadcasted_iota(jnp.int32, (256, 256), 1)
    sums1 = []
    for t in range(4):
        target = sector * 4 + t
        total = None
        for w in range(2):
            channel = chan * 2 + w
            s = source_s[shift_s[channel], target]
            live = size_s[s] * mask_s[channel, target]
            place = jnp.clip(s - (sector * 4 - 4), 0, 11)
            block = gathered[place].reshape(256, 256)
            block = jnp.where(jnp.logical_and(rows < live, cols < live), block, 0.0)
            inner = product(left_h[w, t], left_l[w, t], *split(block))
            term = product(*split(inner), right_h[w, t], right_l[w, t])
            total = term if total is None else total + term
        part[0, t] = total[:, :128].reshape(4, 4, 16, 128)
        part[1, t] = total[:, 128:].reshape(4, 4, 16, 128)
        sent = []
        for d in STEPS:
            sent.append(send(part.at[0, t, x_at[d]], got.at[0, d - 1, t],
                             rs1.at[0, t, d - 1], rr1.at[0, t, d - 1], x_peer[d]))
            sent.append(send(part.at[1, t, every, y_at[d]], got.at[1, d - 1, t],
                             rs1.at[1, t, d - 1], rr1.at[1, t, d - 1], y_peer[d]))
        sums1.append(sent)

    sums2 = []
    for t in range(4):
        for copy in sums1[t]:
            copy.wait_recv()
        mid[0, t] = part[0, t, x] + got[0, 0, t] + got[0, 1, t] + got[0, 2, t]
        mid[1, t] = part[1, t, :, y] + got[1, 0, t] + got[1, 1, t] + got[1, 2, t]
        sent = []
        for d in STEPS:
            sent.append(send(mid.at[0, t, y_at[d]], got2.at[0, d - 1, t],
                             rs2.at[0, t, d - 1], rr2.at[0, t, d - 1], y_peer[d]))
            sent.append(send(mid.at[1, t, x_at[d]], got2.at[1, d - 1, t],
                             rs2.at[1, t, d - 1], rr2.at[1, t, d - 1], x_peer[d]))
        sums2.append(sent)

    row = lax.broadcasted_iota(jnp.int32, (16, 128), 0) + chan * 16
    col = lax.broadcasted_iota(jnp.int32, (16, 128), 1)
    scale = jnp.sqrt(jnp.float32(32))
    for t in range(4):
        for copy in sums2[t]:
            copy.wait_recv()
        live = size_s[sector * 4 + t]
        for half in range(2):
            at = y if half == 0 else x
            total = mid[half, t, at] + got2[half, 0, t] + got2[half, 1, t] + got2[half, 2, t]
            alive = jnp.logical_and(row < live, col + 128 * half < live)
            out[t, :, 128 * half:128 * (half + 1)] = jnp.where(alive, total, 0.0) / scale

    for copy in waits:
        copy.wait_send()


def body(wave, left, right, source, shift, mask, size):
    f32, bf16, i32 = jnp.float32, jnp.bfloat16, jnp.int32
    dma = pltpu.SemaphoreType.DMA
    return pl.pallas_call(
        kernel,
        out_shape=jax.ShapeDtypeStruct((4, 16, 256), f32),
        in_specs=[pl.BlockSpec(memory_space=pl.ANY)] * 7,
        out_specs=pl.BlockSpec(memory_space=pltpu.VMEM),
        scratch_shapes=[
            pltpu.VMEM((12, 4, 4, 16, 256), f32),
            pltpu.VMEM((2, 4, 256, 256), f32),
            pltpu.VMEM((2, 4, 256, 256), f32),
            pltpu.VMEM((2, 4, 256, 256), bf16),
            pltpu.VMEM((2, 4, 256, 256), bf16),
            pltpu.VMEM((2, 4, 256, 256), bf16),
            pltpu.VMEM((2, 4, 256, 256), bf16),
            pltpu.VMEM((2, 4, 4, 4, 16, 128), f32),
            pltpu.VMEM((2, 3, 4, 4, 16, 128), f32),
            pltpu.VMEM((2, 4, 4, 16, 128), f32),
            pltpu.VMEM((2, 3, 4, 16, 128), f32),
            pltpu.SMEM((5, 128), i32),
            pltpu.SMEM((32,), i32),
            pltpu.SMEM((32, 128), i32),
            pltpu.SMEM((128,), i32),
            dma((7,)),
            dma((2, 3)), dma((2, 3)), dma((2, 3)), dma((2, 3)),
            dma((2, 4, 3)), dma((2, 4, 3)), dma((2, 4, 3)), dma((2, 4, 3)),
            dma((1,)), dma((1,)), dma((8,)), dma((8,)),
            dma((2, 4, 3)), dma((2, 4, 3)), dma((2, 4, 3)), dma((2, 4, 3)),
        ],
        compiler_params=pltpu.CompilerParams(
            collective_id=0, has_side_effects=True, vmem_limit_bytes=40 * 2**20
        ),
        cost_estimate=pl.CostEstimate(
            flops=6 * 8 * 2 * 2 * 256**3 // 2, bytes_accessed=5 * 2**20, transcendentals=0
        ),
        name="heff",
    )(wave, left, right, source, shift, mask, size)


def solution(mesh):
    return jax.shard_map(
        body,
        mesh=mesh,
        in_specs=(
            P("sector", "chan", None),
            P("chan", "sector", None, None),
            P("chan", "sector", None, None),
            P(), P(), P(), P(),
        ),
        out_specs=P("sector", "chan", None),
        check_vma=False,
    )
```

time: 202 us -> 47.7 us (0.24)
  the two profiles are of different devices: /device:TPU:1 before, /device:TPU:2 now
where the time goes in v1:
time: 47.7 us; the launch traced here: 47.4 us
  Pallas kernels  40 us (84%)
  local copies, waits for them, and re-layouts  7.36 us (15%)
    pallas_call x1, Pallas kernels, body(): pl.pallas_call(kernel, out_shape=jax.ShapeDtypeStruct((4, 16, 256), f32),...  40 us
    unnamed x15, local copies, waits for them, and re-layouts  7.36 us

profile of v1, /device:TPU:2, one launch (start us, length us, event | category | flops | bytes accessed | tf_op | source)
XLA Modules:
  0.0 47.4 jit_solution(10310526786772938760)
XLA Ops:
  0.0 0.0 copy-start
  0.0 1.6 %copy-done = f32[2,4,256,256]{3,2,1,0:T(8,128)S(1)} copy-done((f32[2,4,256,256]{3,2,1,0:T(8,128)S(1)}, f32[2,4,256,256]{3,2,1,0:T(8,128)}, u32[]{:S(2)}) %copy-start) | copy-done | bytes 2097176
  1.6 0.0 copy-start.1
  1.6 1.6 %copy-done.1 = f32[2,4,256,256]{3,2,1,0:T(8,128)S(1)} copy-done((f32[2,4,256,256]{3,2,1,0:T(8,128)S(1)}, f32[2,4,256,256]{3,2,1,0:T(8,128)}, u32[]{:S(2)}) %copy-start.1) | copy-done | bytes 2097176
  3.2 0.0 copy-start.2
  3.2 0.8 %copy-done.2 = f32[4,16,256]{2,1,0:T(8,128)S(1)} copy-done((f32[4,16,256]{2,1,0:T(8,128)S(1)}, f32[4,16,256]{2,1,0:T(8,128)}, u32[]{:S(2)}) %copy-start.2) | copy-done | bytes 65560
  4.0 0.0 copy-start.3
  4.0 0.7 %copy-done.3 = s32[32,128]{1,0:T(8,128)S(1)} copy-done((s32[32,128]{1,0:T(8,128)S(1)}, s32[32,128]{1,0:T(8,128)}, u32[]{:S(2)}) %copy-start.3) | copy-done | bytes 16408
  4.7 0.0 copy-start.4
  4.7 0.7 %copy-done.4 = s32[5,128]{1,0:T(8,128)S(1)} copy-done((s32[5,128]{1,0:T(8,128)S(1)}, s32[5,128]{1,0:T(8,128)}, u32[]{:S(2)}) %copy-start.4) | copy-done | bytes 2584
  5.4 0.0 copy-start.5
  5.4 0.7 %copy-done.5 = s32[32]{0:T(128)S(1)} copy-done((s32[32]{0:T(128)S(1)}, s32[32]{0:T(128)}, u32[]{:S(2)}) %copy-start.5) | copy-done | bytes 152
  6.1 0.0 copy-start.6
  6.1 0.7 %copy-done.6 = s32[128]{0:T(128)S(1)} copy-done((s32[128]{0:T(128)S(1)}, s32[128]{0:T(128)}, u32[]{:S(2)}) %copy-start.6) | copy-done | bytes 536
  6.7 40.0 %heff.1 = f32[4,16,256]{2,1,0:T(8,128)S(1)} custom-call(f32[4,16,256]{2,1,0:T(8,128)S(1)} %copy-done.2, f32[2,4,256,256]{3,2,1,0:T(8,128)S(1)} %copy-done, f32[2,4,256,256]{3,2,1,0:T(8,128)S(1)} %copy-done.1, s32[5,128]{1,0:T(8,128)S(1)} %copy-done.4, s32[32]{0:T(128)S(1)} %copy-done.5, s32[32,128]{1,0:T(8,128)S(1)} %copy-done.3, s32[128]{0:T(128)S(1)} %copy-done.6), custom_call_target="tpu_custom_call" | custom-call | flops 1610612736 | bytes 5242880 | tf_op jit(solution)/shard_map/heff/pallas_call | solution.py:205
  46.8 0.6 %copy.9 = f32[4,16,256]{2,1,0:T(8,128)} copy(f32[4,16,256]{2,1,0:T(8,128)S(1)} %heff.1) | data formatting | bytes 131072
Async XLA Ops:
  0.0 1.6 %copy-start = (f32[2,4,256,256]{3,2,1,0:T(8,128)S(1)}, f32[2,4,256,256]{3,2,1,0:T(8,128)}, u32[]{:S(2)}) copy-start(f32[2,4,256,256]{3,2,1,0:T(8,128)} %left.1) | copy-start | bytes 6291460
  1.6 1.6 %copy-start.1 = (f32[2,4,256,256]{3,2,1,0:T(8,128)S(1)}, f32[2,4,256,256]{3,2,1,0:T(8,128)}, u32[]{:S(2)}) copy-start(f32[2,4,256,256]{3,2,1,0:T(8,128)} %right.1) | copy-start | bytes 6291460
  3.2 0.8 %copy-start.2 = (f32[4,16,256]{2,1,0:T(8,128)S(1)}, f32[4,16,256]{2,1,0:T(8,128)}, u32[]{:S(2)}) copy-start(f32[4,16,256]{2,1,0:T(8,128)} %wave.1) | copy-start | bytes 196612
  4.0 0.7 %copy-start.3 = (s32[32,128]{1,0:T(8,128)S(1)}, s32[32,128]{1,0:T(8,128)}, u32[]{:S(2)}) copy-start(s32[32,128]{1,0:T(8,128)} %mask.1) | copy-start | bytes 49156
  4.7 0.7 %copy-start.4 = (s32[5,128]{1,0:T(8,128)S(1)}, s32[5,128]{1,0:T(8,128)}, u32[]{:S(2)}) copy-start(s32[5,128]{1,0:T(8,128)} %source.1) | copy-start | bytes 7684
  5.4 0.7 %copy-start.5 = (s32[32]{0:T(128)S(1)}, s32[32]{0:T(128)}, u32[]{:S(2)}) copy-start(s32[32]{0:T(128)} %shift.1) | copy-start | bytes 388
  6.1 0.7 %copy-start.6 = (s32[128]{0:T(128)S(1)}, s32[128]{0:T(128)}, u32[]{:S(2)}) copy-start(s32[128]{0:T(128)} %size.1) | copy-start | bytes 1540

commit v2 on v1

v2 whole, which is shorter than its diff:
```python
import functools

import jax
import jax.numpy as jnp
from jax import lax
from jax.experimental import pallas as pl
from jax.experimental.pallas import tpu as pltpu
from jax.sharding import PartitionSpec as P

MESH = pl.DeviceIdType.MESH
STEPS = (1, 3, 2)


def split(value):
    high = value.astype(jnp.bfloat16)
    low = (value - high.astype(jnp.float32)).astype(jnp.bfloat16)
    return high, low


def product(a_high, a_low, b_high, b_low):
    dot = functools.partial(jnp.dot, preferred_element_type=jnp.float32)
    return dot(a_high, b_high) + dot(a_high, b_low) + dot(a_low, b_high)


def kernel(
    wave, left, right, source, shift, mask, size, out,
    pair0, pair1, next0, next1, left_f, right_f, left_h, left_l, right_h, right_l,
    part0, part1, got, mid, got2, source_s, shift_s, mask_s, size_s,
    local_sem, s1, r1, s2, r2, zs, zr, n2s, n2r, twin_s, twin_r, near_s, near_r,
    ss1, sr1, ss2, sr2,
):
    sector = lax.axis_index("sector")
    chan = lax.axis_index("chan")
    z, core = sector // 2, lax.rem(sector, 2)
    x, y = chan // 4, lax.rem(chan, 4)

    x_at = [lax.rem(x + d, 4) for d in range(4)]
    y_at = [lax.rem(y + d, 4) for d in range(4)]
    x_peer = {d: (sector, x_at[d] * 4 + y) for d in STEPS}
    y_peer = {d: (sector, x * 4 + y_at[d]) for d in STEPS}
    twin = (z * 2 + 1 - core, chan)
    near = (lax.rem(sector + 2 * core - 1 + 32, 32), chan)
    targets = [3 - j + core * (2 * j - 3) for j in range(4)]
    kinds = (pair0.at[core], pair1.at[core])
    ends = (x_at, y_at)
    starts = (y_at, x_at)
    first_peer = (x_peer, y_peer)
    second_peer = (y_peer, x_peer)
    mine = [wave.at[pl.ds(2 * core, 2)], wave.at[pl.ds(2 - 2 * core, 2)]]

    loads = [
        pltpu.make_async_copy(source, source_s, local_sem.at[0]),
        pltpu.make_async_copy(shift, shift_s, local_sem.at[1]),
        pltpu.make_async_copy(mask, mask_s, local_sem.at[2]),
        pltpu.make_async_copy(size, size_s, local_sem.at[3]),
    ]
    left_load = pltpu.make_async_copy(left, left_f, local_sem.at[4])
    right_load = pltpu.make_async_copy(right, right_f, local_sem.at[5])
    keeps = [
        pltpu.make_async_copy(mine[0], pair0.at[core, y, x], local_sem.at[6]),
        pltpu.make_async_copy(mine[1], pair1.at[core, x, y], local_sem.at[7]),
    ]
    for keep in keeps:
        keep.start()

    barrier = pltpu.get_barrier_semaphore()
    partners = [x_peer[d] for d in STEPS] + [y_peer[d] for d in STEPS] + [twin]
    inner_sector = jnp.logical_and(sector > 0, sector < 31)

    @pl.when(inner_sector)
    def _():
        pl.semaphore_signal(barrier, inc=1, device_id=near, device_id_type=MESH)

    for partner in partners:
        pl.semaphore_signal(barrier, inc=1, device_id=partner, device_id_type=MESH)
    pl.semaphore_wait(barrier, len(partners) + inner_sector.astype(jnp.int32))

    sent, sent_near = [], []

    def planned(view, there, send_sem, recv_sem, device):
        return pltpu.make_async_remote_copy(
            src_ref=view, dst_ref=there, send_sem=send_sem, recv_sem=recv_sem,
            device_id=device, device_id_type=MESH,
        )

    def send(*where):
        copy = planned(*where)
        copy.start()
        sent.append(copy)
        return copy

    def send_near(copies):
        @pl.when(inner_sector)
        def _():
            for copy in copies:
                copy.start()

        sent_near.extend(copies)
        return copies

    def wait_near(copies):
        @pl.when(inner_sector)
        def _():
            for copy in copies:
                copy.wait_recv()

    first = {}
    for d in STEPS:
        for kind in range(2):
            first[kind, d] = send(
                mine[kind], kinds[kind].at[starts[kind][0], ends[kind][0]],
                s1.at[kind, d - 1], r1.at[kind, d - 1], first_peer[kind][d])

    nexts = (next0, next1)
    second, over, second_n = {}, {}, {}

    def piece(refs, kind, e):
        return refs[kind].at[starts[kind][0], ends[kind][(4 - e) % 4]]

    def pass_on(kind, e):
        here = piece(kinds, kind, e)
        for d in (2, 1, 3):
            second[kind, e, d] = send(
                here if e else mine[kind], here,
                s2.at[kind, e, d - 1], r2.at[kind, e, d - 1], second_peer[kind][d])

    def cross(kind, e):
        over[kind, e] = planned(piece(kinds, kind, e) if e else mine[kind], piece(nexts, kind, e),
                                zs.at[kind, e], zr.at[kind, e], near)
        send_near([over[kind, e]])

    def pass_on_n(e):
        for kind in range(2):
            here = piece(nexts, kind, e)
            for d in (1, 3):
                second_n[kind, e, d] = planned(
                    here, here, n2s.at[kind, e, d // 2], n2r.at[kind, e, d // 2],
                    second_peer[kind][d])
        copies = [second_n[kind, e, d] for kind in range(2) for d in (1, 3)]

        @pl.when(inner_sector)
        def _():
            for kind in range(2):
                over[kind, e].wait_recv()
                for d in (1, 3):
                    second_n[kind, e, d].start()

        sent_near.extend(copies)

    twins, groups = [], {}

    def group(kind, d):
        at = starts[kind][(4 - d) % 4]
        ref = kinds[kind].at[at]
        if d == 2:
            groups[kind] = planned(
                ref, nexts[kind].at[at], near_s.at[kind], near_r.at[kind], near)
            send_near([groups[kind]])
        twins.append(send(ref, ref, twin_s.at[kind, d], twin_r.at[kind, d], twin))

    for kind in range(2):
        cross(kind, 0)
    for kind in range(2):
        pass_on(kind, 0)
    for load in loads:
        load.start()
    left_load.start()
    right_load.start()
    for d in STEPS:
        for kind in range(2):
            first[kind, d].wait_recv()
            cross(kind, d)
            pass_on(kind, d)
    for keep in keeps:
        keep.wait()
    for kind in range(2):
        group(kind, 0)
    left_load.wait()
    for w in range(2):
        for t in range(4):
            left_h[w, t], left_l[w, t] = split(left_f[w, t])
    for e in (0,) + STEPS:
        pass_on_n(e)
    for d in (2, 1, 3):
        for kind in range(2):
            for e in range(4):
                second[kind, e, d].wait_recv()
            group(kind, d)
        if d == 2:
            right_load.wait()
            for w in range(2):
                for t in range(4):
                    right_h[w, t], right_l[w, t] = split(right_f[w, t])
    for load in loads:
        load.wait()
    for copy in twins:
        copy.wait_recv()

    def assembled(ref, swapped):
        return jnp.concatenate(
            [ref(b, a) if swapped else ref(a, b) for a in range(4) for b in range(4)], axis=0)

    rows = lax.broadcasted_iota(jnp.int32, (256, 256), 0)
    cols = lax.broadcasted_iota(jnp.int32, (256, 256), 1)
    sums1 = []
    for j in range(4):
        if j % 2 == 0:
            kind = j // 2
            wait_near([groups[kind]] + [second_n[kind, e, d] for e in range(4) for d in (1, 3)])
        target = sector * 4 + targets[j]
        total = None
        for w in range(2):
            channel = chan * 2 + w
            s = source_s[shift_s[channel], target]
            live = size_s[s] * mask_s[channel, target]
            place = s - z * 8
            at = jnp.clip(place, 0, 7)
            owner, i, upper = at // 4, lax.rem(at, 2), lax.rem(at, 4) // 2
            block = jnp.where(
                upper == owner,
                assembled(lambda a, b: pair0[owner, a, b, i], True),
                assembled(lambda a, b: pair1[owner, a, b, i], False))
            for i in range(2):
                block = jnp.where(place == i - 2 + 10 * core,
                                  assembled(lambda a, b: next0[a, b, i], True), block)
            if j >= 2:
                for i in range(2):
                    block = jnp.where(place == i - 4 + 14 * core,
                                      assembled(lambda a, b: next1[a, b, i], False), block)
            block = jnp.where(jnp.logical_and(rows < live, cols < live), block, 0.0)
            inner = product(left_h[w, targets[j]], left_l[w, targets[j]], *split(block))
            term = product(*split(inner), right_h[w, targets[j]], right_l[w, targets[j]])
            total = term if total is None else total + term
        for a in range(4):
            for b in range(4):
                r = 64 * a + 16 * b
                part0[j, a, b] = total[r:r + 16, :128]
                part1[j, b, a] = total[r:r + 16, 128:]
        step = []
        for d in STEPS:
            step.append(send(part0.at[j, x_at[d]], got.at[0, d - 1, j],
                             ss1.at[0, j, d - 1], sr1.at[0, j, d - 1], x_peer[d]))
            step.append(send(part1.at[j, y_at[d]], got.at[1, d - 1, j],
                             ss1.at[1, j, d - 1], sr1.at[1, j, d - 1], y_peer[d]))
        sums1.append(step)

    sums2 = []
    for j in range(4):
        for copy in sums1[j]:
            copy.wait_recv()
        mid[0, j] = part0[j, x] + got[0, 0, j] + got[0, 1, j] + got[0, 2, j]
        mid[1, j] = part1[j, y] + got[1, 0, j] + got[1, 1, j] + got[1, 2, j]
        step = []
        for d in STEPS:
            step.append(send(mid.at[0, j, y_at[d]], got2.at[0, d - 1, j],
                             ss2.at[0, j, d - 1], sr2.at[0, j, d - 1], y_peer[d]))
            step.append(send(mid.at[1, j, x_at[d]], got2.at[1, d - 1, j],
                             ss2.at[1, j, d - 1], sr2.at[1, j, d - 1], x_peer[d]))
        sums2.append(step)

    row = lax.broadcasted_iota(jnp.int32, (16, 128), 0) + chan * 16
    col = lax.broadcasted_iota(jnp.int32, (16, 128), 1)
    scale = jnp.sqrt(jnp.float32(32))
    for j in range(4):
        for copy in sums2[j]:
            copy.wait_recv()
        live = size_s[sector * 4 + targets[j]]
        for half, at in ((0, y), (1, x)):
            total = mid[half, j, at] + got2[half, 0, j] + got2[half, 1, j] + got2[half, 2, j]
            alive = jnp.logical_and(row < live, col + 128 * half < live)
            out[targets[j], :, 128 * half:128 * (half + 1)] = jnp.where(alive, total, 0.0) / scale

    for copy in sent:
        copy.wait_send()

    @pl.when(inner_sector)
    def _():
        for copy in sent_near:
            copy.wait_send()


def body(wave, left, right, source, shift, mask, size):
    f32, bf16, i32 = jnp.float32, jnp.bfloat16, jnp.int32
    dma = pltpu.SemaphoreType.DMA
    return pl.pallas_call(
        kernel,
        out_shape=jax.ShapeDtypeStruct((4, 16, 256), f32),
        in_specs=[pl.BlockSpec(memory_space=pl.ANY)] * 7,
        out_specs=pl.BlockSpec(memory_space=pltpu.VMEM),
        scratch_shapes=[
            pltpu.VMEM((2, 4, 4, 2, 16, 256), f32),
            pltpu.VMEM((2, 4, 4, 2, 16, 256), f32),
            pltpu.VMEM((4, 4, 2, 16, 256), f32),
            pltpu.VMEM((4, 4, 2, 16, 256), f32),
            pltpu.VMEM((2, 4, 256, 256), f32),
            pltpu.VMEM((2, 4, 256, 256), f32),
            pltpu.VMEM((2, 4, 256, 256), bf16),
            pltpu.VMEM((2, 4, 256, 256), bf16),
            pltpu.VMEM((2, 4, 256, 256), bf16),
            pltpu.VMEM((2, 4, 256, 256), bf16),
            pltpu.VMEM((4, 4, 4, 16, 128), f32),
            pltpu.VMEM((4, 4, 4, 16, 128), f32),
            pltpu.VMEM((2, 3, 4, 4, 16, 128), f32),
            pltpu.VMEM((2, 4, 4, 16, 128), f32),
            pltpu.VMEM((2, 3, 4, 16, 128), f32),
            pltpu.SMEM((5, 128), i32),
            pltpu.SMEM((32,), i32),
            pltpu.SMEM((32, 128), i32),
            pltpu.SMEM((128,), i32),
            dma((8,)),
            dma((2, 3)), dma((2, 3)), dma((2, 4, 3)), dma((2, 4, 3)),
            dma((2, 4)), dma((2, 4)), dma((2, 4, 2)), dma((2, 4, 2)),
            dma((2, 4)), dma((2, 4)), dma((2,)), dma((2,)),
            dma((2, 4, 3)), dma((2, 4, 3)), dma((2, 4, 3)), dma((2, 4, 3)),
        ],
        compiler_params=pltpu.CompilerParams(
            collective_id=0, has_side_effects=True, vmem_limit_bytes=60 * 2**20
        ),
        cost_estimate=pl.CostEstimate(
            flops=3 * 8 * 2 * 2 * 256**3, bytes_accessed=5 * 2**20, transcendentals=0
        ),
        name="heff",
    )(wave, left, right, source, shift, mask, size)


def solution(mesh):
    return jax.shard_map(
        body,
        mesh=mesh,
        in_specs=(
            P("sector", "chan", None),
            P("chan", "sector", None, None),
            P("chan", "sector", None, None),
            P(), P(), P(), P(),
        ),
        out_specs=P("sector", "chan", None),
        check_vma=False,
    )
```

time: 47.7 us -> 37 us (0.78)
  the two profiles are of different devices: /device:TPU:2 before, /device:TPU:1 now
where the time goes in v2:
time: 37 us; the launch traced here: 36.8 us
  Pallas kernels  35.3 us (95%)
  local copies, waits for them, and re-layouts  1.47 us (4%)
    pallas_call x1, Pallas kernels, body(): pl.pallas_call(kernel, out_shape=jax.ShapeDtypeStruct((4, 16, 256), f32),...  35.3 us
    unnamed x1, local copies, waits for them, and re-layouts  1.47 us

profile of v2, /device:TPU:1, one launch (start us, length us, event | category | flops | bytes accessed | tf_op | source)
XLA Modules:
  0.0 36.8 jit_solution(7562021243657372730)
XLA Ops:
  0.0 35.3 %heff.1 = f32[4,16,256]{2,1,0:T(8,128)} custom-call(f32[4,16,256]{2,1,0:T(8,128)} %wave.1, f32[2,4,256,256]{3,2,1,0:T(8,128)} %left.1, f32[2,4,256,256]{3,2,1,0:T(8,128)} %right.1, s32[5,128]{1,0:T(8,128)} %source.1, s32[32]{0:T(128)} %shift.1, s32[32,128]{1,0:T(8,128)} %mask.1, s32[128]{0:T(128)} %size.1), custom_call_target="tpu_custom_call" | custom-call | flops 1610612736 | bytes 5242880 | tf_op jit(solution)/shard_map/heff/pallas_call | solution.py:285
  35.3 1.5 %copy.9 = f32[4,16,256]{2,1,0:T(8,128)} copy(f32[4,16,256]{2,1,0:T(8,128)} %heff.1) | data formatting | bytes 131072

commit v3 on v2

--- a/solution.py
+++ b/solution.py
@@ -62,6 +62,10 @@
     ]
     for keep in keeps:
         keep.start()
+    left_load.start()
+    right_load.start()
+    for load in loads:
+        load.start()
 
     barrier = pltpu.get_barrier_semaphore()
     partners = [x_peer[d] for d in STEPS] + [y_peer[d] for d in STEPS] + [twin]
@@ -162,10 +166,14 @@
         cross(kind, 0)
     for kind in range(2):
         pass_on(kind, 0)
-    for load in loads:
-        load.start()
-    left_load.start()
-    right_load.start()
+    left_load.wait()
+    for w in range(2):
+        for t in range(4):
+            left_h[w, t], left_l[w, t] = split(left_f[w, t])
+    right_load.wait()
+    for w in range(2):
+        for t in range(4):
+            right_h[w, t], right_l[w, t] = split(right_f[w, t])
     for d in STEPS:
         for kind in range(2):
             first[kind, d].wait_recv()
@@ -175,10 +183,6 @@
         keep.wait()
     for kind in range(2):
         group(kind, 0)
-    left_load.wait()
-    for w in range(2):
-        for t in range(4):
-            left_h[w, t], left_l[w, t] = split(left_f[w, t])
     for e in (0,) + STEPS:
         pass_on_n(e)
     for d in (2, 1, 3):
@@ -186,11 +190,6 @@
             for e in range(4):
                 second[kind, e, d].wait_recv()
             group(kind, d)
-        if d == 2:
-            right_load.wait()
-            for w in range(2):
-                for t in range(4):
-                    right_h[w, t], right_l[w, t] = split(right_f[w, t])
     for load in loads:
         load.wait()
     for copy in twins:
@@ -314,13 +313,13 @@
             dma((2, 4, 3)), dma((2, 4, 3)), dma((2, 4, 3)), dma((2, 4, 3)),
         ],
         compiler_params=pltpu.CompilerParams(
-            collective_id=0, has_side_effects=True, vmem_limit_bytes=60 * 2**20
+            collective_id=0, has_side_effects=True, vmem_limit_bytes=53 * 2**20
         ),
         cost_estimate=pl.CostEstimate(
             flops=3 * 8 * 2 * 2 * 256**3, bytes_accessed=5 * 2**20, transcendentals=0
         ),
         name="heff",
-    )(wave, left, right, source, shift, mask, size)
+    )(*[pltpu.with_memory_space_constraint(v, pltpu.HBM) for v in (wave, left, right, source, shift, mask, size)])
 
 
 def solution(mesh):

time: 37 us -> 35.1 us (0.949)
  Pallas kernels: 35.3 us -> 34.4 us
  local copies, waits for them, and re-layouts: 1.47 us -> 0.63 us
    pallas_call x1, Pallas kernels: 35.3 us -> 34.4 us  [body(): pl.pallas_call(kernel, out_shape=jax.ShapeDtypeStruct((4, 16, 256), f32),...]
    unnamed x1, local copies, waits for them, and re-layouts: 1.47 us -> 0.63 us
where the time goes in v3:
time: 35.1 us; the launch traced here: 35 us
  Pallas kernels  34.4 us (98%)
  local copies, waits for them, and re-layouts  0.63 us (2%)
    pallas_call x1, Pallas kernels, body(): pl.pallas_call(kernel, out_shape=jax.ShapeDtypeStruct((4, 16, 256), f32),...  34.4 us

profile of v3, /device:TPU:1, one launch (start us, length us, event | category | flops | bytes accessed | tf_op | source)
XLA Modules:
  0.0 35.0 jit_solution(84538031452498496)
XLA Ops:
  0.0 34.4 %heff.1 = f32[4,16,256]{2,1,0:T(8,128)S(1)} custom-call(f32[4,16,256]{2,1,0:T(8,128)} %wave.1, f32[2,4,256,256]{3,2,1,0:T(8,128)} %left.1, f32[2,4,256,256]{3,2,1,0:T(8,128)} %right.1, s32[5,128]{1,0:T(8,128)} %source.1, s32[32]{0:T(128)} %shift.1, s32[32,128]{1,0:T(8,128)} %mask.1, s32[128]{0:T(128)} %size.1), custom_call_target="tpu_custom_call" | custom-call | flops 1610612736 | bytes 5242880 | tf_op jit(solution)/shard_map/heff/pallas_call | solution.py:284
  34.4 0.6 %copy.9 = f32[4,16,256]{2,1,0:T(8,128)} copy(f32[4,16,256]{2,1,0:T(8,128)S(1)} %heff.1) | data formatting | bytes 131072

commit v4 on v3

--- a/solution.py
+++ b/solution.py
@@ -46,7 +46,7 @@
     starts = (y_at, x_at)
     first_peer = (x_peer, y_peer)
     second_peer = (y_peer, x_peer)
-    mine = [wave.at[pl.ds(2 * core, 2)], wave.at[pl.ds(2 - 2 * core, 2)]]
+    home = [wave.at[pl.ds(2 * core, 2)], wave.at[pl.ds(2 - 2 * core, 2)]]
 
     loads = [
         pltpu.make_async_copy(source, source_s, local_sem.at[0]),
@@ -57,16 +57,13 @@
     left_load = pltpu.make_async_copy(left, left_f, local_sem.at[4])
     right_load = pltpu.make_async_copy(right, right_f, local_sem.at[5])
     keeps = [
-        pltpu.make_async_copy(mine[0], pair0.at[core, y, x], local_sem.at[6]),
-        pltpu.make_async_copy(mine[1], pair1.at[core, x, y], local_sem.at[7]),
+        pltpu.make_async_copy(home[0], pair0.at[core, y, x], local_sem.at[6]),
+        pltpu.make_async_copy(home[1], pair1.at[core, x, y], local_sem.at[7]),
     ]
     for keep in keeps:
         keep.start()
-    left_load.start()
-    right_load.start()
-    for load in loads:
-        load.start()
-
+
+    mine = [pair0.at[core, y, x], pair1.at[core, x, y]]
     barrier = pltpu.get_barrier_semaphore()
     partners = [x_peer[d] for d in STEPS] + [y_peer[d] for d in STEPS] + [twin]
     inner_sector = jnp.logical_and(sector > 0, sector < 31)
@@ -77,6 +74,8 @@
 
     for partner in partners:
         pl.semaphore_signal(barrier, inc=1, device_id=partner, device_id_type=MESH)
+    for keep in keeps:
+        keep.wait()
     pl.semaphore_wait(barrier, len(partners) + inner_sector.astype(jnp.int32))
 
     sent, sent_near = [], []
@@ -166,6 +165,10 @@
         cross(kind, 0)
     for kind in range(2):
         pass_on(kind, 0)
+    left_load.start()
+    right_load.start()
+    for load in loads:
+        load.start()
     left_load.wait()
     for w in range(2):
         for t in range(4):
@@ -179,8 +182,6 @@
             first[kind, d].wait_recv()
             cross(kind, d)
             pass_on(kind, d)
-    for keep in keeps:
-        keep.wait()
     for kind in range(2):
         group(kind, 0)
     for e in (0,) + STEPS:
@@ -236,7 +237,7 @@
                 part0[j, a, b] = total[r:r + 16, :128]
                 part1[j, b, a] = total[r:r + 16, 128:]
         step = []
-        for d in STEPS:
+        for d in (2, 1, 3):
             step.append(send(part0.at[j, x_at[d]], got.at[0, d - 1, j],
                              ss1.at[0, j, d - 1], sr1.at[0, j, d - 1], x_peer[d]))
             step.append(send(part1.at[j, y_at[d]], got.at[1, d - 1, j],
@@ -245,14 +246,17 @@
 
     sums2 = []
     for j in range(4):
-        for copy in sums1[j]:
+        step = []
+        for copy in sums1[j][0::2]:
             copy.wait_recv()
         mid[0, j] = part0[j, x] + got[0, 0, j] + got[0, 1, j] + got[0, 2, j]
-        mid[1, j] = part1[j, y] + got[1, 0, j] + got[1, 1, j] + got[1, 2, j]
-        step = []
-        for d in STEPS:
+        for d in (2, 1, 3):
             step.append(send(mid.at[0, j, y_at[d]], got2.at[0, d - 1, j],
                              ss2.at[0, j, d - 1], sr2.at[0, j, d - 1], y_peer[d]))
+        for copy in sums1[j][1::2]:
+            copy.wait_recv()
+        mid[1, j] = part1[j, y] + got[1, 0, j] + got[1, 1, j] + got[1, 2, j]
+        for d in (2, 1, 3):
             step.append(send(mid.at[1, j, x_at[d]], got2.at[1, d - 1, j],
                              ss2.at[1, j, d - 1], sr2.at[1, j, d - 1], x_peer[d]))
         sums2.append(step)

time: 35.1 us -> 34.7 us (0.989)
  Pallas kernels: 34.4 us -> 33.9 us
    pallas_call x1, Pallas kernels: 34.4 us -> 33.9 us  [body(): pl.pallas_call(kernel, out_shape=jax.ShapeDtypeStruct((4, 16, 256), f32),...]
where the time goes in v4:
time: 34.7 us; the launch traced here: 34.6 us
  Pallas kernels  33.9 us (98%)
  local copies, waits for them, and re-layouts  0.63 us (2%)
    pallas_call x1, Pallas kernels, body(): pl.pallas_call(kernel, out_shape=jax.ShapeDtypeStruct((4, 16, 256), f32),...  33.9 us

profile of v4, /device:TPU:1, one launch (start us, length us, event | category | flops | bytes accessed | tf_op | source)
XLA Modules:
  0.0 34.6 jit_solution(703170075339527046)
XLA Ops:
  0.0 33.9 %heff.1 = f32[4,16,256]{2,1,0:T(8,128)S(1)} custom-call(f32[4,16,256]{2,1,0:T(8,128)} %wave.1, f32[2,4,256,256]{3,2,1,0:T(8,128)} %left.1, f32[2,4,256,256]{3,2,1,0:T(8,128)} %right.1, s32[5,128]{1,0:T(8,128)} %source.1, s32[32]{0:T(128)} %shift.1, s32[32,128]{1,0:T(8,128)} %mask.1, s32[128]{0:T(128)} %size.1), custom_call_target="tpu_custom_call" | custom-call | flops 1610612736 | bytes 5242880 | tf_op jit(solution)/shard_map/heff/pallas_call | solution.py:288
  33.9 0.6 %copy.9 = f32[4,16,256]{2,1,0:T(8,128)} copy(f32[4,16,256]{2,1,0:T(8,128)S(1)} %heff.1) | data formatting | bytes 131072

commit v5 on v4

--- a/solution.py
+++ b/solution.py
@@ -182,10 +182,13 @@
             first[kind, d].wait_recv()
             cross(kind, d)
             pass_on(kind, d)
+        if d == 1:
+            pass_on_n(0)
+    pass_on_n(1)
+    pass_on_n(3)
     for kind in range(2):
         group(kind, 0)
-    for e in (0,) + STEPS:
-        pass_on_n(e)
+    pass_on_n(2)
     for d in (2, 1, 3):
         for kind in range(2):
             for e in range(4):

time: 34.7 us -> 34.9 us (level)
  no operation moved by 1% of the time
where the time goes in v5:
time: 34.9 us; the launch traced here: 34.8 us
  Pallas kernels  34.1 us (98%)
  local copies, waits for them, and re-layouts  0.63 us (2%)
    pallas_call x1, Pallas kernels, body(): pl.pallas_call(kernel, out_shape=jax.ShapeDtypeStruct((4, 16, 256), f32),...  34.1 us

profile of v5, /device:TPU:1, one launch (start us, length us, event | category | flops | bytes accessed | tf_op | source)
XLA Modules:
  0.0 34.8 jit_solution(10853436416860398368)
XLA Ops:
  0.0 34.1 %heff.1 = f32[4,16,256]{2,1,0:T(8,128)S(1)} custom-call(f32[4,16,256]{2,1,0:T(8,128)} %wave.1, f32[2,4,256,256]{3,2,1,0:T(8,128)} %left.1, f32[2,4,256,256]{3,2,1,0:T(8,128)} %right.1, s32[5,128]{1,0:T(8,128)} %source.1, s32[32]{0:T(128)} %shift.1, s32[32,128]{1,0:T(8,128)} %mask.1, s32[128]{0:T(128)} %size.1), custom_call_target="tpu_custom_call" | custom-call | flops 1610612736 | bytes 5242880 | tf_op jit(solution)/shard_map/heff/pallas_call | solution.py:291
  34.1 0.6 %copy.9 = f32[4,16,256]{2,1,0:T(8,128)} copy(f32[4,16,256]{2,1,0:T(8,128)S(1)} %heff.1) | data formatting | bytes 131072

commit v6 on v4

--- a/solution.py
+++ b/solution.py
@@ -169,14 +169,6 @@
     right_load.start()
     for load in loads:
         load.start()
-    left_load.wait()
-    for w in range(2):
-        for t in range(4):
-            left_h[w, t], left_l[w, t] = split(left_f[w, t])
-    right_load.wait()
-    for w in range(2):
-        for t in range(4):
-            right_h[w, t], right_l[w, t] = split(right_f[w, t])
     for d in STEPS:
         for kind in range(2):
             first[kind, d].wait_recv()
@@ -184,8 +176,16 @@
             pass_on(kind, d)
     for kind in range(2):
         group(kind, 0)
+    left_load.wait()
+    for w in range(2):
+        for t in range(4):
+            left_h[w, t], left_l[w, t] = split(left_f[w, t])
     for e in (0,) + STEPS:
         pass_on_n(e)
+    right_load.wait()
+    for w in range(2):
+        for t in range(4):
+            right_h[w, t], right_l[w, t] = split(right_f[w, t])
     for d in (2, 1, 3):
         for kind in range(2):
             for e in range(4):

time: 34.7 us -> 34.7 us (level)
  no operation moved by 1% of the time
where the time goes in v6:
time: 34.7 us; the launch traced here: 34.6 us
  Pallas kernels  33.9 us (98%)
  local copies, waits for them, and re-layouts  0.63 us (2%)
    pallas_call x1, Pallas kernels, body(): pl.pallas_call(kernel, out_shape=jax.ShapeDtypeStruct((4, 16, 256), f32),...  33.9 us

profile of v6, /device:TPU:1, one launch (start us, length us, event | category | flops | bytes accessed | tf_op | source)
XLA Modules:
  0.0 34.6 jit_solution(14459645396497704431)
XLA Ops:
  0.0 33.9 %heff.1 = f32[4,16,256]{2,1,0:T(8,128)S(1)} custom-call(f32[4,16,256]{2,1,0:T(8,128)} %wave.1, f32[2,4,256,256]{3,2,1,0:T(8,128)} %left.1, f32[2,4,256,256]{3,2,1,0:T(8,128)} %right.1, s32[5,128]{1,0:T(8,128)} %source.1, s32[32]{0:T(128)} %shift.1, s32[32,128]{1,0:T(8,128)} %mask.1, s32[128]{0:T(128)} %size.1), custom_call_target="tpu_custom_call" | custom-call | flops 1610612736 | bytes 5242880 | tf_op jit(solution)/shard_map/heff/pallas_call | solution.py:288
  33.9 0.6 %copy.9 = f32[4,16,256]{2,1,0:T(8,128)} copy(f32[4,16,256]{2,1,0:T(8,128)S(1)} %heff.1) | data formatting | bytes 131072
